TPU v7x, 512 devices: a whole 4x4x16 slice. The times are simulated.
512 devices in a mesh: slab: 16 (over x_lo, y, core), coef: 32 (over x_hi, z).
Axes of the slice: x: 4 (x_hi: 2, x_lo: 2; x = x_hi * 2 + x_lo), y: 4, z: 16, core: 2. Of those that a mesh axis runs over, the one named last changes fastest.
Arguments:
- cotangent: float32 [8192, 4096], P('slab', 'coef'), may hold values from -6 to 6
- transport_state: bfloat16 [8192, 4096], P('slab', 'coef'), may hold values from -6 to 6
- source_state: bfloat16 [8192, 4096], P('slab', 'coef'), may hold values from -6 to 6
- courant: float32 [8192], P('slab'), may hold values from 0.2 to 1.2
- upwind_codes: int32 [8192], P('slab'), may hold values from 0 to 1
- strain_rate: float32 [9, 8192], P(None, ('slab', 'coef')), may hold values from -4 to 4
Outputs:
- adj_source: float32 [8192, 4096], P('slab', 'coef')
- adj_strain: float32 [9, 8192], P(None, ('slab', 'coef'))
- adj_courant: float32 [8192], P(('slab', 'coef'))
All inputs are finite; a program needn't handle non-finite values.
Results may differ from a plain program's by a relative error of at most 0.0003.
Values may be sent and summed in bfloat16 or wider, within the bound.
A program may use at most 64 MiB of HBM per device.

v0:
```python
import math
import jax
import jax.numpy as jnp
from jax import lax
from jax.sharding import PartitionSpec as P

CYZ = 128
NH = 16
QP = 24
K = 4096
section_weights = (0.25, 1.0 / 3.0, 0.5, 1.0)
quad_half = 4.5
fene_limit = 64.0
time_step = 0.005
highest = lax.Precision.HIGHEST
pair_rows = (0, 1, 2, 4, 5, 8)
pair_slots = (0, 1, 2, 1, 3, 4, 2, 4, 5)


def extended(block, sides, width):
    for axis, dim in sides:
        count = lax.axis_size(axis)
        forward = [(i, i + 1) for i in range(count - 1)]
        forward.append((count - 1, 0))
        backward = [(target, source) for source, target in forward]
        low = lax.ppermute(
            lax.slice_in_dim(block, block.shape[dim] - width, None, axis=dim), axis, forward
        )
        high = lax.ppermute(lax.slice_in_dim(block, 0, width, axis=dim), axis, backward)
        block = jnp.concatenate([low, block, high], axis=dim)
    return block


def shifted(shard, axis, by):
    count = lax.axis_size(axis)
    return lax.ppermute(shard, axis, [(i, (i + by) % count) for i in range(count)])


def hermite_table(mode_count, points):
    node_list = quad_half * (2.0 * jnp.arange(points, dtype=jnp.float32) + 1.0 - points) / points
    leading = jnp.exp(-0.5 * node_list * node_list) * math.pi ** (-0.25)
    table_rows = [leading, math.sqrt(2.0) * node_list * leading]
    for degree in range(1, mode_count - 1):
        table_rows.append(
            math.sqrt(2.0 / (degree + 1.0)) * node_list * table_rows[degree]
            - math.sqrt(degree / (degree + 1.0)) * table_rows[degree - 1]
        )
    return (jnp.stack(table_rows[:mode_count]), node_list)


def quadrature_tables(mode_count, points):
    hermite, node_list = hermite_table(mode_count, points)
    cube_shape = (points, points, points)
    coords = (
        jnp.broadcast_to(node_list[:, None, None], cube_shape).reshape(-1),
        jnp.broadcast_to(node_list[None, :, None], cube_shape).reshape(-1),
        jnp.broadcast_to(node_list[None, None, :], cube_shape).reshape(-1),
    )
    spring = (
        1.0 - (coords[0] * coords[0] + coords[1] * coords[1] + coords[2] * coords[2]) / fene_limit
    )
    pair_table = jnp.stack(
        [
            coords[left_dim] * coords[right_dim] / spring
            for left_dim in range(3)
            for right_dim in range(3)
        ]
    )
    return (hermite, pair_table)


def joined_values(coeffs, hermite, kron_table):
    cell_count = coeffs.shape[0]
    mode_count, points = hermite.shape
    inner_part = jnp.dot(
        coeffs.reshape(cell_count * mode_count, mode_count * mode_count),
        kron_table,
        preferred_element_type=jnp.float32,
        precision=highest,
    )
    outer_part = jnp.einsum(
        "cim,ia->cam",
        inner_part.reshape(cell_count, mode_count, points * points),
        hermite,
        precision=highest,
    )
    return outer_part.reshape(cell_count, points**3)


def joined_coefficients(values, hermite, kron_table):
    cell_count = values.shape[0]
    mode_count, points = hermite.shape
    inner_part = jnp.einsum(
        "cam,ia->cim",
        values.reshape(cell_count, points, points * points),
        hermite,
        precision=highest,
    )
    outer_part = jnp.dot(
        inner_part.reshape(cell_count * mode_count, points * points),
        kron_table.T,
        preferred_element_type=jnp.float32,
        precision=highest,
    )
    return outer_part.reshape(cell_count, mode_count**3)


def body(cotangent, transport_state, source_state, courant, upwind_codes, strain_rate):
    row_count, coef_width = cotangent.shape
    plane_count = row_count // CYZ
    grid_shape = (plane_count, CYZ, coef_width)
    speed_grid = courant.reshape(plane_count, CYZ, 1)
    upper_mask = (upwind_codes == 1).astype(jnp.float32).reshape(plane_count, CYZ, 1)
    lower_mask = 1.0 - upper_mask
    initial = transport_state.astype(jnp.float32).reshape(grid_shape)
    differences = []
    section_now = initial
    for section_no in range(4):
        padded = extended(section_now, (("slab", 0),), 1)
        change = lower_mask * (section_now - padded[:-2]) + upper_mask * (padded[2:] - section_now)
        differences.append(change)
        if section_no < 3:
            section_now = initial - section_weights[section_no] * speed_grid * change
    adjoint = cotangent.reshape(grid_shape)
    accumulated = jnp.zeros(grid_shape, jnp.float32)
    speed_part = jnp.zeros((plane_count, CYZ), jnp.float32)
    for section_no in (3, 2, 1, 0):
        speed_part = speed_part - section_weights[section_no] * jnp.sum(
            adjoint * differences[section_no], axis=2
        )
        accumulated = accumulated + adjoint
        weighted = speed_grid * adjoint
        low_part = lower_mask * weighted
        high_part = upper_mask * weighted
        from_above = shifted(low_part[:1], "slab", -1)
        from_below = shifted(high_part[-1:], "slab", 1)
        next_low = jnp.concatenate([low_part[1:], from_above], axis=0)
        prior_high = jnp.concatenate([from_below, high_part[:-1]], axis=0)
        adjoint = -section_weights[section_no] * (low_part - next_low - high_part + prior_high)
    mu_field = (accumulated + adjoint).reshape(row_count, coef_width)
    speed_column = speed_part.reshape(row_count, 1)
    mu_cells, speed_columns = (
        lax.all_to_all(mu_field, "coef", split_axis=0, concat_axis=1, tiled=True),
        lax.all_to_all(speed_column, "coef", split_axis=0, concat_axis=1, tiled=True),
    )
    source_cells = lax.all_to_all(source_state, "coef", split_axis=0, concat_axis=1, tiled=True)
    source_wide = source_cells.astype(jnp.float32)
    adj_courant = jnp.sum(speed_columns, axis=1) / math.sqrt(K)
    hermite, pair_table = quadrature_tables(NH, QP)
    kron_table = (hermite[:, None, :, None] * hermite[None, :, None, :]).reshape(NH * NH, QP * QP)
    weight_cube = (2.0 * quad_half / QP) ** 3
    adj_values = weight_cube * joined_values(mu_cells, hermite, kron_table)
    multiplier = 1.0 + time_step * jnp.einsum(
        "sc,sq->cq", strain_rate, pair_table, precision=highest
    )
    adj_cells = joined_coefficients(multiplier * adj_values, hermite, kron_table)
    unique_table = jnp.stack([pair_table[slot_no] for slot_no in pair_rows])
    source_values = joined_values(source_wide, hermite, kron_table)
    strain_unique = time_step * jnp.einsum(
        "pq,cq->pc", unique_table, adj_values * source_values, precision=highest
    )
    adj_source = lax.all_to_all(adj_cells, "coef", split_axis=1, concat_axis=0, tiled=True)
    adj_strain = jnp.stack([strain_unique[slot_no] for slot_no in pair_slots])
    return (adj_source, adj_strain, adj_courant)


def solution(mesh):
    placed = (
        P("slab", "coef"),
        P("slab", "coef"),
        P("slab", "coef"),
        P("slab"),
        P("slab"),
        P(None, ("slab", "coef")),
    )
    return jax.shard_map(
        body,
        mesh=mesh,
        in_specs=placed,
        out_specs=(P("slab", "coef"), P(None, ("slab", "coef")), P(("slab", "coef"))),
        check_vma=False,
    )
```

profile of v0, /device:TPU:24, one launch (start us, length us, event | category | flops | bytes accessed | tf_op | source)
XLA Modules:
  0.0 190.6 jit_solution(3589017161790618663)
XLA Ops:
  0.7 1.0 convert_element_type.8
  1.7 2.1 %collective-permute-start.9 = (f32[1,128,128]{2,1,0:T(8,128)S(1)}, f32[1,128,128]{2,1,0:T(8,128)S(1)}, u32[]{:S(2)}, u32[]{:S(2)}) collective-permute-start(f32[1,128,128]{2,1,0:T(8,128)S(1)} %get-tuple-element.28), channel_id=1, source_target_pairs={{32,0},{64,32},{96,64},{128,96},{160,128},{192,160},{224,192},{256... | collective-permute-start | bytes 196616 | tf_op jit(solution)/shard_map/ppermute | solution.py:29
  3.8 2.2 %collective-permute-start.8 = (f32[1,128,128]{2,1,0:T(8,128)S(1)}, f32[1,128,128]{2,1,0:T(8,128)S(1)}, u32[]{:S(2)}, u32[]{:S(2)}) collective-permute-start(f32[1,128,128]{2,1,0:T(8,128)S(1)} %get-tuple-element.27), channel_id=1, source_target_pairs={{0,32},{32,64},{64,96},{96,128},{128,160},{160,192},{192,224},{224... | collective-permute-start | bytes 196616 | tf_op jit(solution)/shard_map/ppermute | solution.py:26
  6.0 0.7 broadcast_multiply_fusion.7
  6.7 0.7 broadcast_multiply_fusion.12
  9.2 0.7 fusion.41
  9.9 0.8 fusion.45
  11.1 3.3 %collective-permute-start.11 = (f32[1,128,128]{2,1,0:T(8,128)S(1)}, f32[1,128,128]{2,1,0:T(8,128)S(1)}, u32[]{:S(2)}, u32[]{:S(2)}) collective-permute-start(f32[1,128,128]{2,1,0:T(8,128)S(1)} %get-tuple-element.26), channel_id=1, source_target_pairs={{32,0},{64,32},{96,64},{128,96},{160,128},{192,160},{224,192},{256... | collective-permute-start | bytes 196616 | tf_op jit(solution)/shard_map/ppermute | solution.py:29
  14.4 3.7 %collective-permute-start.10 = (f32[1,128,128]{2,1,0:T(8,128)S(1)}, f32[1,128,128]{2,1,0:T(8,128)S(1)}, u32[]{:S(2)}, u32[]{:S(2)}) collective-permute-start(f32[1,128,128]{2,1,0:T(8,128)S(1)} %get-tuple-element.25), channel_id=1, source_target_pairs={{0,32},{32,64},{64,96},{96,128},{128,160},{160,192},{192,224},{224... | collective-permute-start | bytes 196616 | tf_op jit(solution)/shard_map/ppermute | solution.py:26
  18.7 1.4 collective-permute-done.10
  20.3 1.9 %collective-permute-start.13 = (f32[1,128,128]{2,1,0:T(8,128)S(1)}, f32[1,128,128]{2,1,0:T(8,128)S(1)}, u32[]{:S(2)}, u32[]{:S(2)}) collective-permute-start(f32[1,128,128]{2,1,0:T(8,128)S(1)} %get-tuple-element.24), channel_id=1, source_target_pairs={{32,0},{64,32},{96,64},{128,96},{160,128},{192,160},{224,192},{256... | collective-permute-start | bytes 196616 | tf_op jit(solution)/shard_map/ppermute | solution.py:29
  22.2 5.2 %collective-permute-start.12 = (f32[1,128,128]{2,1,0:T(8,128)S(1)}, f32[1,128,128]{2,1,0:T(8,128)S(1)}, u32[]{:S(2)}, u32[]{:S(2)}) collective-permute-start(f32[1,128,128]{2,1,0:T(8,128)S(1)} %get-tuple-element.23), channel_id=1, source_target_pairs={{0,32},{32,64},{64,96},{96,128},{128,160},{160,192},{192,224},{224... | collective-permute-start | bytes 196616 | tf_op jit(solution)/shard_map/ppermute | solution.py:26
  28.7 6.8 %collective-permute-start.1 = (f32[1,128,128]{2,1,0:T(8,128)S(1)}, f32[1,128,128]{2,1,0:T(8,128)S(1)}, u32[]{:S(2)}, u32[]{:S(2)}) collective-permute-start(f32[1,128,128]{2,1,0:T(8,128)S(1)} %slice.173), channel_id=1, source_target_pairs={{0,32},{32,64},{64,96},{96,128},{128,160},{160,192},{192,224},{224... | collective-permute-start | bytes 196616 | tf_op jit(solution)/shard_map/ppermute | solution.py:36
  35.5 1.9 %collective-permute-start = (f32[1,128,128]{2,1,0:T(8,128)S(1)}, f32[1,128,128]{2,1,0:T(8,128)S(1)}, u32[]{:S(2)}, u32[]{:S(2)}) collective-permute-start(f32[1,128,128]{2,1,0:T(8,128)S(1)} %slice.172), channel_id=1, source_target_pairs={{0,480},{32,0},{64,32},{96,64},{128,96},{160,128},{192,160},{224,1... | collective-permute-start | bytes 196616 | tf_op jit(solution)/shard_map/ppermute | solution.py:36
  37.5 1.9 %collective-permute-start.15 = (f32[1,128,128]{2,1,0:T(8,128)S(1)}, f32[1,128,128]{2,1,0:T(8,128)S(1)}, u32[]{:S(2)}, u32[]{:S(2)}) collective-permute-start(f32[1,128,128]{2,1,0:T(8,128)S(1)} %get-tuple-element.22), channel_id=1, source_target_pairs={{32,0},{64,32},{96,64},{128,96},{160,128},{192,160},{224,192},{256... | collective-permute-start | bytes 196616 | tf_op jit(solution)/shard_map/ppermute | solution.py:29
  39.4 6.4 %collective-permute-start.14 = (f32[1,128,128]{2,1,0:T(8,128)S(1)}, f32[1,128,128]{2,1,0:T(8,128)S(1)}, u32[]{:S(2)}, u32[]{:S(2)}) collective-permute-start(f32[1,128,128]{2,1,0:T(8,128)S(1)} %get-tuple-element.21), channel_id=1, source_target_pairs={{0,32},{32,64},{64,96},{96,128},{128,160},{160,192},{192,224},{224... | collective-permute-start | bytes 196616 | tf_op jit(solution)/shard_map/ppermute | solution.py:26
  46.3 5.8 %collective-permute-start.3 = (f32[1,128,128]{2,1,0:T(8,128)S(1)}, f32[1,128,128]{2,1,0:T(8,128)S(1)}, u32[]{:S(2)}, u32[]{:S(2)}) collective-permute-start(f32[1,128,128]{2,1,0:T(8,128)S(1)} %slice.177), channel_id=1, source_target_pairs={{0,32},{32,64},{64,96},{96,128},{128,160},{160,192},{192,224},{224... | collective-permute-start | bytes 196616 | tf_op jit(solution)/shard_map/ppermute | solution.py:36
  52.0 1.9 %collective-permute-start.2 = (f32[1,128,128]{2,1,0:T(8,128)S(1)}, f32[1,128,128]{2,1,0:T(8,128)S(1)}, u32[]{:S(2)}, u32[]{:S(2)}) collective-permute-start(f32[1,128,128]{2,1,0:T(8,128)S(1)} %slice.176), channel_id=1, source_target_pairs={{0,480},{32,0},{64,32},{96,64},{128,96},{160,128},{192,160},{224,1... | collective-permute-start | bytes 196616 | tf_op jit(solution)/shard_map/ppermute | solution.py:36
  54.6 1.2 collective-permute-done.2
  56.7 6.3 %collective-permute-start.5 = (f32[1,128,128]{2,1,0:T(8,128)S(1)}, f32[1,128,128]{2,1,0:T(8,128)S(1)}, u32[]{:S(2)}, u32[]{:S(2)}) collective-permute-start(f32[1,128,128]{2,1,0:T(8,128)S(1)} %slice.181), channel_id=1, source_target_pairs={{0,32},{32,64},{64,96},{96,128},{128,160},{160,192},{192,224},{224... | collective-permute-start | bytes 196616 | tf_op jit(solution)/shard_map/ppermute | solution.py:36
  63.0 1.9 %collective-permute-start.4 = (f32[1,128,128]{2,1,0:T(8,128)S(1)}, f32[1,128,128]{2,1,0:T(8,128)S(1)}, u32[]{:S(2)}, u32[]{:S(2)}) collective-permute-start(f32[1,128,128]{2,1,0:T(8,128)S(1)} %slice.180), channel_id=1, source_target_pairs={{0,480},{32,0},{64,32},{96,64},{128,96},{160,128},{192,160},{224,1... | collective-permute-start | bytes 196616 | tf_op jit(solution)/shard_map/ppermute | solution.py:36
  65.0 1.8 collective-permute-done.4
  67.6 5.8 %collective-permute-start.7 = (f32[1,128,128]{2,1,0:T(8,128)S(1)}, f32[1,128,128]{2,1,0:T(8,128)S(1)}, u32[]{:S(2)}, u32[]{:S(2)}) collective-permute-start(f32[1,128,128]{2,1,0:T(8,128)S(1)} %slice.185), channel_id=1, source_target_pairs={{0,32},{32,64},{64,96},{96,128},{128,160},{160,192},{192,224},{224... | collective-permute-start | bytes 196616 | tf_op jit(solution)/shard_map/ppermute | solution.py:36
  73.4 1.9 %collective-permute-start.6 = (f32[1,128,128]{2,1,0:T(8,128)S(1)}, f32[1,128,128]{2,1,0:T(8,128)}, u32[]{:S(2)}, u32[]{:S(2)}) collective-permute-start(f32[1,128,128]{2,1,0:T(8,128)S(1)} %slice.184), channel_id=1, source_target_pairs={{0,480},{32,0},{64,32},{96,64},{128,96},{160,128},{192,160},{224,1... | collective-permute-start | bytes 196616 | tf_op jit(solution)/shard_map/ppermute | solution.py:36
  75.4 0.7 sub.1010
  76.1 17.9 %all-to-all-start.3 = ((f32[32,16,1]{1,2,0:T(1,128)}), f32[32,16,1]{1,2,0:T(1,128)S(1)}, u32[]{:S(2)}, u32[]{:S(2)}) async-start(f32[32,16,1]{1,2,0:T(1,128)} %bitcast.29), calls=%async_computation.3 | async-start | bytes 32768 | tf_op jit(solution)/shard_map/all_to_all | solution.py:144
  94.1 14.7 %all-to-all-done.3 = f32[32,16,1]{1,2,0:T(1,128)S(1)} async-done(((f32[32,16,1]{1,2,0:T(1,128)}), f32[32,16,1]{1,2,0:T(1,128)S(1)}, u32[]{:S(2)}, u32[]{:S(2)}) %all-to-all-start.3) | async-done | bytes 2080 | tf_op jit(solution)/shard_map/all_to_all | solution.py:144
  108.8 3.9 %all-to-all-start.2 = ((bf16[32,16,128]{2,1,0:T(8,128)(2,1)}), bf16[32,16,128]{2,1,0:T(8,128)(2,1)S(1)}, u32[]{:S(2)}, u32[]{:S(2)}) async-start(bf16[32,16,128]{2,1,0:T(8,128)(2,1)} %bitcast.21), calls=%async_computation.2 | async-start | bytes 262144 | tf_op jit(solution)/shard_map/all_to_all | solution.py:146
  112.8 0.9 pad_maximum_fusion.14
  113.6 1.2 fusion.30
  114.8 15.6 %all-to-all-done.2 = bf16[32,16,128]{2,1,0:T(8,128)(2,1)S(1)} async-done(((bf16[32,16,128]{2,1,0:T(8,128)(2,1)}), bf16[32,16,128]{2,1,0:T(8,128)(2,1)S(1)}, u32[]{:S(2)}, u32[]{:S(2)}) %all-to-all-start.2) | async-done | bytes 131104 | tf_op jit(solution)/shard_map/all_to_all | solution.py:146
  130.5 4.1 %all-to-all-start = ((f32[32,16,128]{2,1,0:T(8,128)}), f32[32,16,128]{2,1,0:T(8,128)S(1)}, u32[]{:S(2)}, u32[]{:S(2)}) async-start(f32[32,16,128]{2,1,0:T(8,128)} %bitcast.13), calls=%async_computation | async-start | bytes 524288 | tf_op jit(solution)/shard_map/all_to_all | solution.py:143
  134.6 3.6 %stack.10 = f32[9,13824]{1,0:T(8,128)} concatenate(f32[1,13824]{1,0:T(1,128)} %get-tuple-element.33, f32[1,13824]{1,0:T(1,128)S(1)} %get-tuple-element.32, f32[1,13824]{1,0:T(1,128)S(1)} %get-tuple-element.31, f32[1,13824]{1,0:T(1,128)S(1)} %get-tuple-element.32, f32[1,13824]{1,0:T(1,128)S(1)} %get-tuple-element.30, f32[1,13824]{1,0:T(1,128)S(1)} %get-tuple-element.29, ...), dimensions={0} | concatenate | bytes 995328 | tf_op jit(solution)/shard_map/stack | solution.py:62
  138.2 1.2 stack.11
  139.9 1.8 mul.3480
  141.7 0.8 reduce_sum.49
  143.1 13.5 %all-to-all-done = f32[32,16,128]{2,1,0:T(8,128)S(1)} async-done(((f32[32,16,128]{2,1,0:T(8,128)}), f32[32,16,128]{2,1,0:T(8,128)S(1)}, u32[]{:S(2)}, u32[]{:S(2)}) %all-to-all-start) | async-done | bytes 262176 | tf_op jit(solution)/shard_map/all_to_all | solution.py:143
  156.8 1.9 fusion.5
  158.7 1.0 fusion.3
  159.9 2.2 %fusion.2 = f32[16,13824]{1,0:T(8,128)S(1)} fusion(f32[16,13824]{1,0:T(8,128)S(1)} %mul.3484, f32[9,13824]{1,0:T(8,128)} %stack.10, f32[9,16]{1,0:T(8,128)S(1)} %copy-done), kind=kOutput, calls=%fused_computation.3 | convolution fusion | flops 24551424 | bytes 2267712 | tf_op jit(solution)/shard_map/sc,sq->cq/dot_general | solution.py:153
  163.1 0.8 fusion.48
  164.0 0.9 copy.17
  164.9 3.9 %all-to-all-start.1 = ((f32[16,32,128]{2,0,1:T(8,128)}), f32[16,32,128]{2,0,1:T(8,128)S(1)}, u32[]{:S(2)}, u32[]{:S(2)}) async-start(f32[16,32,128]{2,0,1:T(8,128)} %copy.17), calls=%async_computation.1 | async-start | bytes 524288 | tf_op jit(solution)/shard_map/all_to_all | solution.py:162
  169.7 1.0 convolution_bitcast_fusion
  170.9 2.2 %convolution_multiply_fusion.2 = f32[6,16]{1,0:T(8,128)S(1)} fusion(f32[6,13824]{1,0:T(8,128)} %stack.11, f32[16,13824]{1,0:T(8,128)S(1)} %mul.3484, f32[16,13824]{1,0:T(8,128)S(1)} %reshape.613), kind=kOutput, calls=%fused_computation.9 | convolution fusion | flops 16146528 | bytes 2101632 | tf_op jit(solution)/shard_map/pq,cq->pc/dot_general | solution.py:159
  173.1 2.0 %stack.12 = f32[9,16]{1,0:T(8,128)} concatenate(f32[3,16]{1,0:T(4,128)S(1)} %slice.148, f32[1,16]{1,0:T(1,128)S(1)} %get-tuple-element.38, f32[2,16]{1,0:T(2,128)S(1)} %get-tuple-element.36, f32[1,16]{1,0:T(1,128)S(1)} %get-tuple-element.37, f32[2,16]{1,0:T(2,128)S(1)} %get-tuple-element.35), dimensions={0} | concatenate | bytes 1152 | tf_op jit(solution)/shard_map/stack | solution.py:163
  175.1 14.8 %all-to-all-done.1 = f32[16,32,128]{2,0,1:T(8,128)S(1)} async-done(((f32[16,32,128]{2,0,1:T(8,128)}), f32[16,32,128]{2,0,1:T(8,128)S(1)}, u32[]{:S(2)}, u32[]{:S(2)}) %all-to-all-start.1) | async-done | bytes 262176 | tf_op jit(solution)/shard_map/all_to_all | solution.py:162
  189.9 0.7 copy.24
  (116 shorter events, 10.7 us)
Async XLA Ops:
  0.6 159.3 %copy-start = (f32[9,16]{1,0:T(8,128)S(1)}, f32[9,16]{1,0:T(8,128)}, u32[]{:S(2)}) copy-start(f32[9,16]{1,0:T(8,128)} %param.11) | copy-start | bytes 1732
  0.6 19.4 %copy-start.3 = (bf16[512,128]{1,0:T(8,128)(2,1)S(1)}, bf16[512,128]{1,0:T(8,128)(2,1)}, u32[]{:S(2)}) copy-start(bf16[512,128]{1,0:T(8,128)(2,1)} %param.7) | copy-start | bytes 393220
  0.7 10.1 %copy-start.8 = (s32[512]{0:T(512)S(1)}, s32[512]{0:T(512)}, u32[]{:S(2)}) copy-start(s32[512]{0:T(512)} %param.10) | copy-start | bytes 6148
  1.7 9.1 %collective-permute-start.9 = (f32[1,128,128]{2,1,0:T(8,128)S(1)}, f32[1,128,128]{2,1,0:T(8,128)S(1)}, u32[]{:S(2)}, u32[]{:S(2)}) collective-permute-start(f32[1,128,128]{2,1,0:T(8,128)S(1)} %get-tuple-element.28), channel_id=1, source_target_pairs={{32,0},{64,32},{96,64},{128,96},{160,128},{192,160},{224,192},{256... | collective-permute-start | bytes 196616 | tf_op jit(solution)/shard_map/ppermute | solution.py:29
  3.8 7.0 %collective-permute-start.8 = (f32[1,128,128]{2,1,0:T(8,128)S(1)}, f32[1,128,128]{2,1,0:T(8,128)S(1)}, u32[]{:S(2)}, u32[]{:S(2)}) collective-permute-start(f32[1,128,128]{2,1,0:T(8,128)S(1)} %get-tuple-element.27), channel_id=1, source_target_pairs={{0,32},{32,64},{64,96},{96,128},{128,160},{160,192},{192,224},{224... | collective-permute-start | bytes 196616 | tf_op jit(solution)/shard_map/ppermute | solution.py:26
  7.6 20.7 %copy-start.2 = (f32[512,128]{1,0:T(8,128)S(1)}, f32[512,128]{1,0:T(8,128)}, u32[]{:S(2)}) copy-start(f32[512,128]{1,0:T(8,128)} %param.6) | copy-start | bytes 786436
  7.6 20.7 %copy-start.7 = (f32[512]{0:T(512)S(1)}, f32[512]{0:T(512)}, u32[]{:S(2)}) copy-start(f32[512]{0:T(512)} %param.9) | copy-start | bytes 6148
  11.1 7.6 %collective-permute-start.11 = (f32[1,128,128]{2,1,0:T(8,128)S(1)}, f32[1,128,128]{2,1,0:T(8,128)S(1)}, u32[]{:S(2)}, u32[]{:S(2)}) collective-permute-start(f32[1,128,128]{2,1,0:T(8,128)S(1)} %get-tuple-element.26), channel_id=1, source_target_pairs={{32,0},{64,32},{96,64},{128,96},{160,128},{192,160},{224,192},{256... | collective-permute-start | bytes 196616 | tf_op jit(solution)/shard_map/ppermute | solution.py:29
  14.4 5.6 %collective-permute-start.10 = (f32[1,128,128]{2,1,0:T(8,128)S(1)}, f32[1,128,128]{2,1,0:T(8,128)S(1)}, u32[]{:S(2)}, u32[]{:S(2)}) collective-permute-start(f32[1,128,128]{2,1,0:T(8,128)S(1)} %get-tuple-element.25), channel_id=1, source_target_pairs={{0,32},{32,64},{64,96},{96,128},{128,160},{160,192},{192,224},{224... | collective-permute-start | bytes 196616 | tf_op jit(solution)/shard_map/ppermute | solution.py:26
  20.3 7.7 %collective-permute-start.13 = (f32[1,128,128]{2,1,0:T(8,128)S(1)}, f32[1,128,128]{2,1,0:T(8,128)S(1)}, u32[]{:S(2)}, u32[]{:S(2)}) collective-permute-start(f32[1,128,128]{2,1,0:T(8,128)S(1)} %get-tuple-element.24), channel_id=1, source_target_pairs={{32,0},{64,32},{96,64},{128,96},{160,128},{192,160},{224,192},{256... | collective-permute-start | bytes 196616 | tf_op jit(solution)/shard_map/ppermute | solution.py:29
  22.2 6.1 %collective-permute-start.12 = (f32[1,128,128]{2,1,0:T(8,128)S(1)}, f32[1,128,128]{2,1,0:T(8,128)S(1)}, u32[]{:S(2)}, u32[]{:S(2)}) collective-permute-start(f32[1,128,128]{2,1,0:T(8,128)S(1)} %get-tuple-element.23), channel_id=1, source_target_pairs={{0,32},{32,64},{64,96},{96,128},{128,160},{160,192},{192,224},{224... | collective-permute-start | bytes 196616 | tf_op jit(solution)/shard_map/ppermute | solution.py:26
  28.7 17.1 %collective-permute-start.1 = (f32[1,128,128]{2,1,0:T(8,128)S(1)}, f32[1,128,128]{2,1,0:T(8,128)S(1)}, u32[]{:S(2)}, u32[]{:S(2)}) collective-permute-start(f32[1,128,128]{2,1,0:T(8,128)S(1)} %slice.173), channel_id=1, source_target_pairs={{0,32},{32,64},{64,96},{96,128},{128,160},{160,192},{192,224},{224... | collective-permute-start | bytes 196616 | tf_op jit(solution)/shard_map/ppermute | solution.py:36
  35.5 10.3 %collective-permute-start = (f32[1,128,128]{2,1,0:T(8,128)S(1)}, f32[1,128,128]{2,1,0:T(8,128)S(1)}, u32[]{:S(2)}, u32[]{:S(2)}) collective-permute-start(f32[1,128,128]{2,1,0:T(8,128)S(1)} %slice.172), channel_id=1, source_target_pairs={{0,480},{32,0},{64,32},{96,64},{128,96},{160,128},{192,160},{224,1... | collective-permute-start | bytes 196616 | tf_op jit(solution)/shard_map/ppermute | solution.py:36
  37.5 17.1 %collective-permute-start.15 = (f32[1,128,128]{2,1,0:T(8,128)S(1)}, f32[1,128,128]{2,1,0:T(8,128)S(1)}, u32[]{:S(2)}, u32[]{:S(2)}) collective-permute-start(f32[1,128,128]{2,1,0:T(8,128)S(1)} %get-tuple-element.22), channel_id=1, source_target_pairs={{32,0},{64,32},{96,64},{128,96},{160,128},{192,160},{224,192},{256... | collective-permute-start | bytes 196616 | tf_op jit(solution)/shard_map/ppermute | solution.py:29
  39.4 15.2 %collective-permute-start.14 = (f32[1,128,128]{2,1,0:T(8,128)S(1)}, f32[1,128,128]{2,1,0:T(8,128)S(1)}, u32[]{:S(2)}, u32[]{:S(2)}) collective-permute-start(f32[1,128,128]{2,1,0:T(8,128)S(1)} %get-tuple-element.21), channel_id=1, source_target_pairs={{0,32},{32,64},{64,96},{96,128},{128,160},{160,192},{192,224},{224... | collective-permute-start | bytes 196616 | tf_op jit(solution)/shard_map/ppermute | solution.py:26
  46.3 8.4 %collective-permute-start.3 = (f32[1,128,128]{2,1,0:T(8,128)S(1)}, f32[1,128,128]{2,1,0:T(8,128)S(1)}, u32[]{:S(2)}, u32[]{:S(2)}) collective-permute-start(f32[1,128,128]{2,1,0:T(8,128)S(1)} %slice.177), channel_id=1, source_target_pairs={{0,32},{32,64},{64,96},{96,128},{128,160},{160,192},{192,224},{224... | collective-permute-start | bytes 196616 | tf_op jit(solution)/shard_map/ppermute | solution.py:36
  52.0 3.8 %collective-permute-start.2 = (f32[1,128,128]{2,1,0:T(8,128)S(1)}, f32[1,128,128]{2,1,0:T(8,128)S(1)}, u32[]{:S(2)}, u32[]{:S(2)}) collective-permute-start(f32[1,128,128]{2,1,0:T(8,128)S(1)} %slice.176), channel_id=1, source_target_pairs={{0,480},{32,0},{64,32},{96,64},{128,96},{160,128},{192,160},{224,1... | collective-permute-start | bytes 196616 | tf_op jit(solution)/shard_map/ppermute | solution.py:36
  56.7 8.3 %collective-permute-start.5 = (f32[1,128,128]{2,1,0:T(8,128)S(1)}, f32[1,128,128]{2,1,0:T(8,128)S(1)}, u32[]{:S(2)}, u32[]{:S(2)}) collective-permute-start(f32[1,128,128]{2,1,0:T(8,128)S(1)} %slice.181), channel_id=1, source_target_pairs={{0,32},{32,64},{64,96},{96,128},{128,160},{160,192},{192,224},{224... | collective-permute-start | bytes 196616 | tf_op jit(solution)/shard_map/ppermute | solution.py:36
  63.0 3.8 %collective-permute-start.4 = (f32[1,128,128]{2,1,0:T(8,128)S(1)}, f32[1,128,128]{2,1,0:T(8,128)S(1)}, u32[]{:S(2)}, u32[]{:S(2)}) collective-permute-start(f32[1,128,128]{2,1,0:T(8,128)S(1)} %slice.180), channel_id=1, source_target_pairs={{0,480},{32,0},{64,32},{96,64},{128,96},{160,128},{192,160},{224,1... | collective-permute-start | bytes 196616 | tf_op jit(solution)/shard_map/ppermute | solution.py:36
  67.6 45.1 %collective-permute-start.7 = (f32[1,128,128]{2,1,0:T(8,128)S(1)}, f32[1,128,128]{2,1,0:T(8,128)S(1)}, u32[]{:S(2)}, u32[]{:S(2)}) collective-permute-start(f32[1,128,128]{2,1,0:T(8,128)S(1)} %slice.185), channel_id=1, source_target_pairs={{0,32},{32,64},{64,96},{96,128},{128,160},{160,192},{192,224},{224... | collective-permute-start | bytes 196616 | tf_op jit(solution)/shard_map/ppermute | solution.py:36
  73.4 39.3 %collective-permute-start.6 = (f32[1,128,128]{2,1,0:T(8,128)S(1)}, f32[1,128,128]{2,1,0:T(8,128)}, u32[]{:S(2)}, u32[]{:S(2)}) collective-permute-start(f32[1,128,128]{2,1,0:T(8,128)S(1)} %slice.184), channel_id=1, source_target_pairs={{0,480},{32,0},{64,32},{96,64},{128,96},{160,128},{192,160},{224,1... | collective-permute-start | bytes 196616 | tf_op jit(solution)/shard_map/ppermute | solution.py:36
  76.1 32.7 %all-to-all-start.3 = ((f32[32,16,1]{1,2,0:T(1,128)}), f32[32,16,1]{1,2,0:T(1,128)S(1)}, u32[]{:S(2)}, u32[]{:S(2)}) async-start(f32[32,16,1]{1,2,0:T(1,128)} %bitcast.29), calls=%async_computation.3 | async-start | bytes 32768 | tf_op jit(solution)/shard_map/all_to_all | solution.py:144
  94.1 44.1 %copy-start.4 = (f32[1,13824]{1,0:T(1,128)S(1)}, f32[1,13824]{1,0:T(1,128)}, u32[]{:S(2)}) copy-start(f32[1,13824]{1,0:T(1,128)} %get-tuple-element.33) | copy-start | bytes 165892
  94.1 44.1 %copy-start.5 = (f32[1,13824]{1,0:T(1,128)S(1)}, f32[1,13824]{1,0:T(1,128)}, u32[]{:S(2)}) copy-start(f32[1,13824]{1,0:T(1,128)} %get-tuple-element.9) | copy-start | bytes 165892
  108.8 21.7 %copy-start.6 = (f32[32,16,1]{1,2,0:T(1,128)}, f32[32,16,1]{1,2,0:T(1,128)S(1)}, u32[]{:S(2)}) copy-start(f32[32,16,1]{1,2,0:T(1,128)S(1)} %all-to-all-done.3) | copy-start | bytes 6148
  108.8 21.7 %all-to-all-start.2 = ((bf16[32,16,128]{2,1,0:T(8,128)(2,1)}), bf16[32,16,128]{2,1,0:T(8,128)(2,1)S(1)}, u32[]{:S(2)}, u32[]{:S(2)}) async-start(bf16[32,16,128]{2,1,0:T(8,128)(2,1)} %bitcast.21), calls=%async_computation.2 | async-start | bytes 262144 | tf_op jit(solution)/shard_map/all_to_all | solution.py:146
  112.7 26.8 %copy-start.9 = (f32[1,24]{1,0:T(1,128)S(1)}, f32[1,24]{1,0:T(1,128)}, u32[]{:S(2)}) copy-start(f32[1,24]{1,0:T(1,128)} %get-tuple-element.69) | copy-start | bytes 292
  112.7 26.8 %copy-start.10 = (f32[1,24]{1,0:T(1,128)S(1)}, f32[1,24]{1,0:T(1,128)}, u32[]{:S(2)}) copy-start(f32[1,24]{1,0:T(1,128)} %get-tuple-element.70) | copy-start | bytes 292
  112.7 26.8 %copy-start.11 = (f32[1,24]{1,0:T(1,128)S(1)}, f32[1,24]{1,0:T(1,128)}, u32[]{:S(2)}) copy-start(f32[1,24]{1,0:T(1,128)} %get-tuple-element.67) | copy-start | bytes 292
  112.7 26.8 %copy-start.12 = (f32[1,24]{1,0:T(1,128)S(1)}, f32[1,24]{1,0:T(1,128)}, u32[]{:S(2)}) copy-start(f32[1,24]{1,0:T(1,128)} %get-tuple-element.68) | copy-start | bytes 292
  112.7 26.8 %copy-start.13 = (f32[1,24]{1,0:T(1,128)S(1)}, f32[1,24]{1,0:T(1,128)}, u32[]{:S(2)}) copy-start(f32[1,24]{1,0:T(1,128)} %get-tuple-element.65) | copy-start | bytes 292
  112.7 26.8 %copy-start.14 = (f32[1,24]{1,0:T(1,128)S(1)}, f32[1,24]{1,0:T(1,128)}, u32[]{:S(2)}) copy-start(f32[1,24]{1,0:T(1,128)} %get-tuple-element.66) | copy-start | bytes 292
  130.5 26.1 %all-to-all-start = ((f32[32,16,128]{2,1,0:T(8,128)}), f32[32,16,128]{2,1,0:T(8,128)S(1)}, u32[]{:S(2)}, u32[]{:S(2)}) async-start(f32[32,16,128]{2,1,0:T(8,128)} %bitcast.13), calls=%async_computation | async-start | bytes 524288 | tf_op jit(solution)/shard_map/all_to_all | solution.py:143
  159.9 3.2 %copy-start.1 = (f32[256,576]{1,0:T(8,128)S(1)}, f32[256,576]{1,0:T(8,128)}, u32[]{:S(2)}) copy-start(f32[256,576]{1,0:T(8,128)} %mul.3480) | copy-start | bytes 1769476
  164.9 25.1 %all-to-all-start.1 = ((f32[16,32,128]{2,0,1:T(8,128)}), f32[16,32,128]{2,0,1:T(8,128)S(1)}, u32[]{:S(2)}, u32[]{:S(2)}) async-start(f32[16,32,128]{2,0,1:T(8,128)} %copy.17), calls=%async_computation.1 | async-start | bytes 524288 | tf_op jit(solution)/shard_map/all_to_all | solution.py:162
where the time goes:
time: 192 us; the launch traced here: 191 us
  starting transfers between devices  88.8 us (46%)
  waiting for transfers between devices  63.4 us (33%)
  local copies, waits for them, and re-layouts  14 us (7%)
  other arithmetic  12.6 us (7%)
  matrix products  10.4 us (5%)
    ppermute x8, starting transfers between devices, shifted(): lax.ppermute(shard, axis, [(i, (i + by) % count) for i in range(count)])  32.3 us
    all_to_all x1, starting transfers between devices, body(): lax.all_to_all(speed_column, 'coef', split_axis=0, concat_axis=1, tiled=T...  17.9 us
    ppermute x4, starting transfers between devices, extended(): lax.ppermute(lax.slice_in_dim(block, block.shape[dim] - width, None, axis...  17.5 us
    all_to_all x1, waiting for transfers between devices, body(): lax.all_to_all(source_state, 'coef', split_axis=0, concat_axis=1, tiled=T...  15.6 us
    all_to_all x1, waiting for transfers between devices, body(): lax.all_to_all(adj_cells, 'coef', split_axis=1, concat_axis=0, tiled=True)  14.8 us
    all_to_all x1, waiting for transfers between devices, body(): lax.all_to_all(speed_column, 'coef', split_axis=0, concat_axis=1, tiled=T...  14.7 us
    all_to_all x1, waiting for transfers between devices, body(): lax.all_to_all(mu_field, 'coef', split_axis=0, concat_axis=1, tiled=True)  13.5 us
    ppermute x4, starting transfers between devices, extended(): lax.ppermute(lax.slice_in_dim(block, 0, width, axis=dim), axis, backward)  9.26 us
  transfers between devices with their start and end apart: 20, of which 8 were waited for; matrix products, arithmetic and copies ran while one was open for 13% of the time, Pallas kernels for 0%

commit v1 on v0

--- a/solution.py
+++ b/solution.py
@@ -159,7 +159,16 @@
     strain_unique = time_step * jnp.einsum(
         "pq,cq->pc", unique_table, adj_values * source_values, precision=highest
     )
-    adj_source = lax.all_to_all(adj_cells, "coef", split_axis=1, concat_axis=0, tiled=True)
+    _state_clusters = lambda sample, dim_k, d0: jnp.concatenate(
+        jax.lax.all_to_all(
+            jnp.stack(jnp.split(sample, jax.lax.axis_size("coef"), dim_k), 0),
+            axis_name="coef",
+            split_axis=0,
+            concat_axis=0,
+        ),
+        d0,
+    )
+    adj_source = _state_clusters(adj_cells, 1, 0)
     adj_strain = jnp.stack([strain_unique[slot_no] for slot_no in pair_slots])
     return (adj_source, adj_strain, adj_courant)
 

time: 192 us -> 210 us (1.094)
  local copies, waits for them, and re-layouts: 14 us -> 32.4 us
    unnamed x31 -> x62, local copies, waits for them, and re-layouts: 0.78 us -> 19.4 us
  transfers between devices with their start and end apart: 20 -> 20, of which waited for: 8 -> 8; matrix products, arithmetic and copies ran while one was open for 13% -> 12% of each run, Pallas kernels for 0% -> 0%
where the time goes in v1:
time: 210 us; the launch traced here: 209 us
  starting transfers between devices  88.8 us (42%)
  waiting for transfers between devices  63.4 us (30%)
  local copies, waits for them, and re-layouts  32.4 us (15%)
  other arithmetic  12.6 us (6%)
  matrix products  10.4 us (5%)
    ppermute x8, starting transfers between devices, shifted(): lax.ppermute(shard, axis, [(i, (i + by) % count) for i in range(count)])  32.3 us
    unnamed x62, local copies, waits for them, and re-layouts  19.4 us
    all_to_all x1, starting transfers between devices, body(): lax.all_to_all(speed_column, 'coef', split_axis=0, concat_axis=1, tiled=T...  17.9 us
    ppermute x4, starting transfers between devices, extended(): lax.ppermute(lax.slice_in_dim(block, block.shape[dim] - width, None, axis...  17.5 us
    all_to_all x1, waiting for transfers between devices, body(): lax.all_to_all(source_state, 'coef', split_axis=0, concat_axis=1, tiled=T...  15.6 us
    all_to_all x1, waiting for transfers between devices, body(): jax.lax.all_to_all(jnp.stack(jnp.split(sample, jax.lax.axis_size('coef'),...  14.8 us
    all_to_all x1, waiting for transfers between devices, body(): lax.all_to_all(speed_column, 'coef', split_axis=0, concat_axis=1, tiled=T...  14.7 us
    all_to_all x1, waiting for transfers between devices, body(): lax.all_to_all(mu_field, 'coef', split_axis=0, concat_axis=1, tiled=True)  13.5 us
  transfers between devices with their start and end apart: 20, of which 8 were waited for; matrix products, arithmetic and copies ran while one was open for 12% of the time, Pallas kernels for 0%

profile of v1, /device:TPU:24, one launch (start us, length us, event | category | flops | bytes accessed | tf_op | source)
XLA Modules:
  0.0 209.0 jit_solution(12393909474459514668)
XLA Ops:
  0.7 1.0 convert_element_type.8
  1.7 2.1 %collective-permute-start.9 = (f32[1,128,128]{2,1,0:T(8,128)S(1)}, f32[1,128,128]{2,1,0:T(8,128)S(1)}, u32[]{:S(2)}, u32[]{:S(2)}) collective-permute-start(f32[1,128,128]{2,1,0:T(8,128)S(1)} %get-tuple-element.28), channel_id=1, source_target_pairs={{32,0},{64,32},{96,64},{128,96},{160,128},{192,160},{224,192},{256... | collective-permute-start | bytes 196616 | tf_op jit(solution)/shard_map/ppermute | solution.py:29
  3.8 2.2 %collective-permute-start.8 = (f32[1,128,128]{2,1,0:T(8,128)S(1)}, f32[1,128,128]{2,1,0:T(8,128)S(1)}, u32[]{:S(2)}, u32[]{:S(2)}) collective-permute-start(f32[1,128,128]{2,1,0:T(8,128)S(1)} %get-tuple-element.27), channel_id=1, source_target_pairs={{0,32},{32,64},{64,96},{96,128},{128,160},{160,192},{192,224},{224... | collective-permute-start | bytes 196616 | tf_op jit(solution)/shard_map/ppermute | solution.py:26
  6.0 0.7 broadcast_multiply_fusion.7
  6.7 0.7 broadcast_multiply_fusion.12
  9.2 0.7 fusion.41
  9.9 0.8 fusion.45
  11.1 3.3 %collective-permute-start.11 = (f32[1,128,128]{2,1,0:T(8,128)S(1)}, f32[1,128,128]{2,1,0:T(8,128)S(1)}, u32[]{:S(2)}, u32[]{:S(2)}) collective-permute-start(f32[1,128,128]{2,1,0:T(8,128)S(1)} %get-tuple-element.26), channel_id=1, source_target_pairs={{32,0},{64,32},{96,64},{128,96},{160,128},{192,160},{224,192},{256... | collective-permute-start | bytes 196616 | tf_op jit(solution)/shard_map/ppermute | solution.py:29
  14.4 3.7 %collective-permute-start.10 = (f32[1,128,128]{2,1,0:T(8,128)S(1)}, f32[1,128,128]{2,1,0:T(8,128)S(1)}, u32[]{:S(2)}, u32[]{:S(2)}) collective-permute-start(f32[1,128,128]{2,1,0:T(8,128)S(1)} %get-tuple-element.25), channel_id=1, source_target_pairs={{0,32},{32,64},{64,96},{96,128},{128,160},{160,192},{192,224},{224... | collective-permute-start | bytes 196616 | tf_op jit(solution)/shard_map/ppermute | solution.py:26
  18.7 1.4 collective-permute-done.10
  20.3 1.9 collective-permute-start.13
  22.2 5.2 %collective-permute-start.12 = (f32[1,128,128]{2,1,0:T(8,128)S(1)}, f32[1,128,128]{2,1,0:T(8,128)S(1)}, u32[]{:S(2)}, u32[]{:S(2)}) collective-permute-start(f32[1,128,128]{2,1,0:T(8,128)S(1)} %get-tuple-element.23), channel_id=1, source_target_pairs={{0,32},{32,64},{64,96},{96,128},{128,160},{160,192},{192,224},{224... | collective-permute-start | bytes 196616 | tf_op jit(solution)/shard_map/ppermute | solution.py:26
  28.7 6.8 %collective-permute-start.1 = (f32[1,128,128]{2,1,0:T(8,128)S(1)}, f32[1,128,128]{2,1,0:T(8,128)S(1)}, u32[]{:S(2)}, u32[]{:S(2)}) collective-permute-start(f32[1,128,128]{2,1,0:T(8,128)S(1)} %slice.173), channel_id=1, source_target_pairs={{0,32},{32,64},{64,96},{96,128},{128,160},{160,192},{192,224},{224... | collective-permute-start | bytes 196616 | tf_op jit(solution)/shard_map/ppermute | solution.py:36
  35.5 1.9 collective-permute-start
  37.5 1.9 collective-permute-start.15
  39.4 6.4 %collective-permute-start.14 = (f32[1,128,128]{2,1,0:T(8,128)S(1)}, f32[1,128,128]{2,1,0:T(8,128)S(1)}, u32[]{:S(2)}, u32[]{:S(2)}) collective-permute-start(f32[1,128,128]{2,1,0:T(8,128)S(1)} %get-tuple-element.21), channel_id=1, source_target_pairs={{0,32},{32,64},{64,96},{96,128},{128,160},{160,192},{192,224},{224... | collective-permute-start | bytes 196616 | tf_op jit(solution)/shard_map/ppermute | solution.py:26
  46.3 5.8 %collective-permute-start.3 = (f32[1,128,128]{2,1,0:T(8,128)S(1)}, f32[1,128,128]{2,1,0:T(8,128)S(1)}, u32[]{:S(2)}, u32[]{:S(2)}) collective-permute-start(f32[1,128,128]{2,1,0:T(8,128)S(1)} %slice.177), channel_id=1, source_target_pairs={{0,32},{32,64},{64,96},{96,128},{128,160},{160,192},{192,224},{224... | collective-permute-start | bytes 196616 | tf_op jit(solution)/shard_map/ppermute | solution.py:36
  52.0 1.9 collective-permute-start.2
  54.6 1.2 collective-permute-done.2
  56.7 6.3 %collective-permute-start.5 = (f32[1,128,128]{2,1,0:T(8,128)S(1)}, f32[1,128,128]{2,1,0:T(8,128)S(1)}, u32[]{:S(2)}, u32[]{:S(2)}) collective-permute-start(f32[1,128,128]{2,1,0:T(8,128)S(1)} %slice.181), channel_id=1, source_target_pairs={{0,32},{32,64},{64,96},{96,128},{128,160},{160,192},{192,224},{224... | collective-permute-start | bytes 196616 | tf_op jit(solution)/shard_map/ppermute | solution.py:36
  63.0 1.9 collective-permute-start.4
  65.0 1.8 collective-permute-done.4
  67.6 5.8 %collective-permute-start.7 = (f32[1,128,128]{2,1,0:T(8,128)S(1)}, f32[1,128,128]{2,1,0:T(8,128)S(1)}, u32[]{:S(2)}, u32[]{:S(2)}) collective-permute-start(f32[1,128,128]{2,1,0:T(8,128)S(1)} %slice.185), channel_id=1, source_target_pairs={{0,32},{32,64},{64,96},{96,128},{128,160},{160,192},{192,224},{224... | collective-permute-start | bytes 196616 | tf_op jit(solution)/shard_map/ppermute | solution.py:36
  73.4 1.9 collective-permute-start.6
  75.4 0.7 sub.1010
  76.1 17.9 %all-to-all-start.3 = ((f32[32,16,1]{1,2,0:T(1,128)}), f32[32,16,1]{1,2,0:T(1,128)S(1)}, u32[]{:S(2)}, u32[]{:S(2)}) async-start(f32[32,16,1]{1,2,0:T(1,128)} %bitcast.60), calls=%async_computation.3 | async-start | bytes 32768 | tf_op jit(solution)/shard_map/all_to_all | solution.py:144
  94.1 14.7 %all-to-all-done.3 = f32[32,16,1]{1,2,0:T(1,128)S(1)} async-done(((f32[32,16,1]{1,2,0:T(1,128)}), f32[32,16,1]{1,2,0:T(1,128)S(1)}, u32[]{:S(2)}, u32[]{:S(2)}) %all-to-all-start.3) | async-done | bytes 2080 | tf_op jit(solution)/shard_map/all_to_all | solution.py:144
  108.8 3.9 %all-to-all-start.2 = ((bf16[32,16,128]{2,1,0:T(8,128)(2,1)}), bf16[32,16,128]{2,1,0:T(8,128)(2,1)S(1)}, u32[]{:S(2)}, u32[]{:S(2)}) async-start(bf16[32,16,128]{2,1,0:T(8,128)(2,1)} %bitcast.52), calls=%async_computation.2 | async-start | bytes 262144 | tf_op jit(solution)/shard_map/all_to_all | solution.py:146
  112.8 0.9 pad_maximum_fusion.14
  113.6 1.2 fusion.30
  114.8 15.6 %all-to-all-done.2 = bf16[32,16,128]{2,1,0:T(8,128)(2,1)S(1)} async-done(((bf16[32,16,128]{2,1,0:T(8,128)(2,1)}), bf16[32,16,128]{2,1,0:T(8,128)(2,1)S(1)}, u32[]{:S(2)}, u32[]{:S(2)}) %all-to-all-start.2) | async-done | bytes 131104 | tf_op jit(solution)/shard_map/all_to_all | solution.py:146
  130.5 4.1 %all-to-all-start = ((f32[32,16,128]{2,1,0:T(8,128)}), f32[32,16,128]{2,1,0:T(8,128)S(1)}, u32[]{:S(2)}, u32[]{:S(2)}) async-start(f32[32,16,128]{2,1,0:T(8,128)} %bitcast.13), calls=%async_computation | async-start | bytes 524288 | tf_op jit(solution)/shard_map/all_to_all | solution.py:143
  134.6 3.6 %stack.138 = f32[9,13824]{1,0:T(8,128)} concatenate(f32[1,13824]{1,0:T(1,128)} %get-tuple-element.33, f32[1,13824]{1,0:T(1,128)S(1)} %get-tuple-element.32, f32[1,13824]{1,0:T(1,128)S(1)} %get-tuple-element.31, f32[1,13824]{1,0:T(1,128)S(1)} %get-tuple-element.32, f32[1,13824]{1,0:T(1,128)S(1)} %get-tuple-element.30, f32[1,13824]{1,0:T(1,128)S(1)} %get-tuple-element.29, ...), dimensions={0} | concatenate | bytes 995328 | tf_op jit(solution)/shard_map/stack | solution.py:62
  138.2 1.2 stack.172
  139.9 1.8 mul.3480
  141.7 0.8 reduce_sum.49
  143.1 13.5 %all-to-all-done = f32[32,16,128]{2,1,0:T(8,128)S(1)} async-done(((f32[32,16,128]{2,1,0:T(8,128)}), f32[32,16,128]{2,1,0:T(8,128)S(1)}, u32[]{:S(2)}, u32[]{:S(2)}) %all-to-all-start) | async-done | bytes 262176 | tf_op jit(solution)/shard_map/all_to_all | solution.py:143
  156.8 1.9 fusion.5
  158.7 1.0 fusion.3
  159.9 2.2 %fusion.2 = f32[16,13824]{1,0:T(8,128)S(1)} fusion(f32[16,13824]{1,0:T(8,128)S(1)} %mul.3484, f32[9,13824]{1,0:T(8,128)} %stack.138, f32[9,16]{1,0:T(8,128)S(1)} %copy-done), kind=kOutput, calls=%fused_computation.3 | convolution fusion | flops 24551424 | bytes 2267712 | tf_op jit(solution)/shard_map/sc,sq->cq/dot_general | solution.py:153
  162.4 0.7 fusion.36
  163.1 0.8 fusion.48
  183.2 3.9 %all-to-all-start.1 = ((f32[32,16,128]{2,1,0:T(8,128)}), f32[32,16,128]{2,1,0:T(8,128)S(1)}, u32[]{:S(2)}, u32[]{:S(2)}) async-start(f32[32,16,128]{2,1,0:T(8,128)} %constant_dynamic-update-slice_fusion), calls=%async_computation.1 | async-start | bytes 524288 | tf_op jit(solution)/shard_map/all_to_all | solution.py:163
  188.0 1.0 convolution_bitcast_fusion
  189.3 2.2 %convolution_multiply_fusion.2 = f32[6,16]{1,0:T(8,128)S(1)} fusion(f32[6,13824]{1,0:T(8,128)} %stack.172, f32[16,13824]{1,0:T(8,128)S(1)} %mul.3484, f32[16,13824]{1,0:T(8,128)S(1)} %reshape.616), kind=kOutput, calls=%fused_computation.9 | convolution fusion | flops 16146528 | bytes 2101632 | tf_op jit(solution)/shard_map/pq,cq->pc/dot_general | solution.py:159
  191.5 2.0 stack.173
  193.5 14.8 %all-to-all-done.1 = f32[32,16,128]{2,1,0:T(8,128)S(1)} async-done(((f32[32,16,128]{2,1,0:T(8,128)}), f32[32,16,128]{2,1,0:T(8,128)S(1)}, u32[]{:S(2)}, u32[]{:S(2)}) %all-to-all-start.1) | async-done | bytes 262176 | tf_op jit(solution)/shard_map/all_to_all | solution.py:163
  208.3 0.7 copy.52
  (147 shorter events, 29.2 us)
Async XLA Ops:
  0.6 159.3 %copy-start = (f32[9,16]{1,0:T(8,128)S(1)}, f32[9,16]{1,0:T(8,128)}, u32[]{:S(2)}) copy-start(f32[9,16]{1,0:T(8,128)} %param.11) | copy-start | bytes 1732
  0.6 19.4 %copy-start.3 = (bf16[512,128]{1,0:T(8,128)(2,1)S(1)}, bf16[512,128]{1,0:T(8,128)(2,1)}, u32[]{:S(2)}) copy-start(bf16[512,128]{1,0:T(8,128)(2,1)} %param.7) | copy-start | bytes 393220
  0.7 10.1 %copy-start.8 = (s32[512]{0:T(512)S(1)}, s32[512]{0:T(512)}, u32[]{:S(2)}) copy-start(s32[512]{0:T(512)} %param.10) | copy-start | bytes 6148
  1.7 9.1 %collective-permute-start.9 = (f32[1,128,128]{2,1,0:T(8,128)S(1)}, f32[1,128,128]{2,1,0:T(8,128)S(1)}, u32[]{:S(2)}, u32[]{:S(2)}) collective-permute-start(f32[1,128,128]{2,1,0:T(8,128)S(1)} %get-tuple-element.28), channel_id=1, source_target_pairs={{32,0},{64,32},{96,64},{128,96},{160,128},{192,160},{224,192},{256... | collective-permute-start | bytes 196616 | tf_op jit(solution)/shard_map/ppermute | solution.py:29
  3.8 7.0 %collective-permute-start.8 = (f32[1,128,128]{2,1,0:T(8,128)S(1)}, f32[1,128,128]{2,1,0:T(8,128)S(1)}, u32[]{:S(2)}, u32[]{:S(2)}) collective-permute-start(f32[1,128,128]{2,1,0:T(8,128)S(1)} %get-tuple-element.27), channel_id=1, source_target_pairs={{0,32},{32,64},{64,96},{96,128},{128,160},{160,192},{192,224},{224... | collective-permute-start | bytes 196616 | tf_op jit(solution)/shard_map/ppermute | solution.py:26
  7.6 20.7 %copy-start.2 = (f32[512,128]{1,0:T(8,128)S(1)}, f32[512,128]{1,0:T(8,128)}, u32[]{:S(2)}) copy-start(f32[512,128]{1,0:T(8,128)} %param.6) | copy-start | bytes 786436
  7.6 20.7 %copy-start.7 = (f32[512]{0:T(512)S(1)}, f32[512]{0:T(512)}, u32[]{:S(2)}) copy-start(f32[512]{0:T(512)} %param.9) | copy-start | bytes 6148
  11.1 7.6 %collective-permute-start.11 = (f32[1,128,128]{2,1,0:T(8,128)S(1)}, f32[1,128,128]{2,1,0:T(8,128)S(1)}, u32[]{:S(2)}, u32[]{:S(2)}) collective-permute-start(f32[1,128,128]{2,1,0:T(8,128)S(1)} %get-tuple-element.26), channel_id=1, source_target_pairs={{32,0},{64,32},{96,64},{128,96},{160,128},{192,160},{224,192},{256... | collective-permute-start | bytes 196616 | tf_op jit(solution)/shard_map/ppermute | solution.py:29
  14.4 5.6 %collective-permute-start.10 = (f32[1,128,128]{2,1,0:T(8,128)S(1)}, f32[1,128,128]{2,1,0:T(8,128)S(1)}, u32[]{:S(2)}, u32[]{:S(2)}) collective-permute-start(f32[1,128,128]{2,1,0:T(8,128)S(1)} %get-tuple-element.25), channel_id=1, source_target_pairs={{0,32},{32,64},{64,96},{96,128},{128,160},{160,192},{192,224},{224... | collective-permute-start | bytes 196616 | tf_op jit(solution)/shard_map/ppermute | solution.py:26
  20.3 7.7 %collective-permute-start.13 = (f32[1,128,128]{2,1,0:T(8,128)S(1)}, f32[1,128,128]{2,1,0:T(8,128)S(1)}, u32[]{:S(2)}, u32[]{:S(2)}) collective-permute-start(f32[1,128,128]{2,1,0:T(8,128)S(1)} %get-tuple-element.24), channel_id=1, source_target_pairs={{32,0},{64,32},{96,64},{128,96},{160,128},{192,160},{224,192},{256... | collective-permute-start | bytes 196616 | tf_op jit(solution)/shard_map/ppermute | solution.py:29
  22.2 6.1 %collective-permute-start.12 = (f32[1,128,128]{2,1,0:T(8,128)S(1)}, f32[1,128,128]{2,1,0:T(8,128)S(1)}, u32[]{:S(2)}, u32[]{:S(2)}) collective-permute-start(f32[1,128,128]{2,1,0:T(8,128)S(1)} %get-tuple-element.23), channel_id=1, source_target_pairs={{0,32},{32,64},{64,96},{96,128},{128,160},{160,192},{192,224},{224... | collective-permute-start | bytes 196616 | tf_op jit(solution)/shard_map/ppermute | solution.py:26
  28.7 17.1 %collective-permute-start.1 = (f32[1,128,128]{2,1,0:T(8,128)S(1)}, f32[1,128,128]{2,1,0:T(8,128)S(1)}, u32[]{:S(2)}, u32[]{:S(2)}) collective-permute-start(f32[1,128,128]{2,1,0:T(8,128)S(1)} %slice.173), channel_id=1, source_target_pairs={{0,32},{32,64},{64,96},{96,128},{128,160},{160,192},{192,224},{224... | collective-permute-start | bytes 196616 | tf_op jit(solution)/shard_map/ppermute | solution.py:36
  35.5 10.3 %collective-permute-start = (f32[1,128,128]{2,1,0:T(8,128)S(1)}, f32[1,128,128]{2,1,0:T(8,128)S(1)}, u32[]{:S(2)}, u32[]{:S(2)}) collective-permute-start(f32[1,128,128]{2,1,0:T(8,128)S(1)} %slice.172), channel_id=1, source_target_pairs={{0,480},{32,0},{64,32},{96,64},{128,96},{160,128},{192,160},{224,1... | collective-permute-start | bytes 196616 | tf_op jit(solution)/shard_map/ppermute | solution.py:36
  37.5 17.1 %collective-permute-start.15 = (f32[1,128,128]{2,1,0:T(8,128)S(1)}, f32[1,128,128]{2,1,0:T(8,128)S(1)}, u32[]{:S(2)}, u32[]{:S(2)}) collective-permute-start(f32[1,128,128]{2,1,0:T(8,128)S(1)} %get-tuple-element.22), channel_id=1, source_target_pairs={{32,0},{64,32},{96,64},{128,96},{160,128},{192,160},{224,192},{256... | collective-permute-start | bytes 196616 | tf_op jit(solution)/shard_map/ppermute | solution.py:29
  39.4 15.2 %collective-permute-start.14 = (f32[1,128,128]{2,1,0:T(8,128)S(1)}, f32[1,128,128]{2,1,0:T(8,128)S(1)}, u32[]{:S(2)}, u32[]{:S(2)}) collective-permute-start(f32[1,128,128]{2,1,0:T(8,128)S(1)} %get-tuple-element.21), channel_id=1, source_target_pairs={{0,32},{32,64},{64,96},{96,128},{128,160},{160,192},{192,224},{224... | collective-permute-start | bytes 196616 | tf_op jit(solution)/shard_map/ppermute | solution.py:26
  46.3 8.4 %collective-permute-start.3 = (f32[1,128,128]{2,1,0:T(8,128)S(1)}, f32[1,128,128]{2,1,0:T(8,128)S(1)}, u32[]{:S(2)}, u32[]{:S(2)}) collective-permute-start(f32[1,128,128]{2,1,0:T(8,128)S(1)} %slice.177), channel_id=1, source_target_pairs={{0,32},{32,64},{64,96},{96,128},{128,160},{160,192},{192,224},{224... | collective-permute-start | bytes 196616 | tf_op jit(solution)/shard_map/ppermute | solution.py:36
  52.0 3.8 %collective-permute-start.2 = (f32[1,128,128]{2,1,0:T(8,128)S(1)}, f32[1,128,128]{2,1,0:T(8,128)S(1)}, u32[]{:S(2)}, u32[]{:S(2)}) collective-permute-start(f32[1,128,128]{2,1,0:T(8,128)S(1)} %slice.176), channel_id=1, source_target_pairs={{0,480},{32,0},{64,32},{96,64},{128,96},{160,128},{192,160},{224,1... | collective-permute-start | bytes 196616 | tf_op jit(solution)/shard_map/ppermute | solution.py:36
  56.7 8.3 %collective-permute-start.5 = (f32[1,128,128]{2,1,0:T(8,128)S(1)}, f32[1,128,128]{2,1,0:T(8,128)S(1)}, u32[]{:S(2)}, u32[]{:S(2)}) collective-permute-start(f32[1,128,128]{2,1,0:T(8,128)S(1)} %slice.181), channel_id=1, source_target_pairs={{0,32},{32,64},{64,96},{96,128},{128,160},{160,192},{192,224},{224... | collective-permute-start | bytes 196616 | tf_op jit(solution)/shard_map/ppermute | solution.py:36
  63.0 3.8 %collective-permute-start.4 = (f32[1,128,128]{2,1,0:T(8,128)S(1)}, f32[1,128,128]{2,1,0:T(8,128)S(1)}, u32[]{:S(2)}, u32[]{:S(2)}) collective-permute-start(f32[1,128,128]{2,1,0:T(8,128)S(1)} %slice.180), channel_id=1, source_target_pairs={{0,480},{32,0},{64,32},{96,64},{128,96},{160,128},{192,160},{224,1... | collective-permute-start | bytes 196616 | tf_op jit(solution)/shard_map/ppermute | solution.py:36
  67.6 45.1 %collective-permute-start.7 = (f32[1,128,128]{2,1,0:T(8,128)S(1)}, f32[1,128,128]{2,1,0:T(8,128)S(1)}, u32[]{:S(2)}, u32[]{:S(2)}) collective-permute-start(f32[1,128,128]{2,1,0:T(8,128)S(1)} %slice.185), channel_id=1, source_target_pairs={{0,32},{32,64},{64,96},{96,128},{128,160},{160,192},{192,224},{224... | collective-permute-start | bytes 196616 | tf_op jit(solution)/shard_map/ppermute | solution.py:36
  73.4 39.3 %collective-permute-start.6 = (f32[1,128,128]{2,1,0:T(8,128)S(1)}, f32[1,128,128]{2,1,0:T(8,128)}, u32[]{:S(2)}, u32[]{:S(2)}) collective-permute-start(f32[1,128,128]{2,1,0:T(8,128)S(1)} %slice.184), channel_id=1, source_target_pairs={{0,480},{32,0},{64,32},{96,64},{128,96},{160,128},{192,160},{224,1... | collective-permute-start | bytes 196616 | tf_op jit(solution)/shard_map/ppermute | solution.py:36
  76.1 32.7 %all-to-all-start.3 = ((f32[32,16,1]{1,2,0:T(1,128)}), f32[32,16,1]{1,2,0:T(1,128)S(1)}, u32[]{:S(2)}, u32[]{:S(2)}) async-start(f32[32,16,1]{1,2,0:T(1,128)} %bitcast.60), calls=%async_computation.3 | async-start | bytes 32768 | tf_op jit(solution)/shard_map/all_to_all | solution.py:144
  94.1 44.1 %copy-start.4 = (f32[1,13824]{1,0:T(1,128)S(1)}, f32[1,13824]{1,0:T(1,128)}, u32[]{:S(2)}) copy-start(f32[1,13824]{1,0:T(1,128)} %get-tuple-element.33) | copy-start | bytes 165892
  94.1 44.1 %copy-start.5 = (f32[1,13824]{1,0:T(1,128)S(1)}, f32[1,13824]{1,0:T(1,128)}, u32[]{:S(2)}) copy-start(f32[1,13824]{1,0:T(1,128)} %get-tuple-element.9) | copy-start | bytes 165892
  108.8 21.7 %copy-start.6 = (f32[32,16,1]{1,2,0:T(1,128)}, f32[32,16,1]{1,2,0:T(1,128)S(1)}, u32[]{:S(2)}) copy-start(f32[32,16,1]{1,2,0:T(1,128)S(1)} %all-to-all-done.3) | copy-start | bytes 6148
  108.8 21.7 %all-to-all-start.2 = ((bf16[32,16,128]{2,1,0:T(8,128)(2,1)}), bf16[32,16,128]{2,1,0:T(8,128)(2,1)S(1)}, u32[]{:S(2)}, u32[]{:S(2)}) async-start(bf16[32,16,128]{2,1,0:T(8,128)(2,1)} %bitcast.52), calls=%async_computation.2 | async-start | bytes 262144 | tf_op jit(solution)/shard_map/all_to_all | solution.py:146
  112.7 26.8 %copy-start.9 = (f32[1,24]{1,0:T(1,128)S(1)}, f32[1,24]{1,0:T(1,128)}, u32[]{:S(2)}) copy-start(f32[1,24]{1,0:T(1,128)} %get-tuple-element.69) | copy-start | bytes 292
  112.7 26.8 %copy-start.10 = (f32[1,24]{1,0:T(1,128)S(1)}, f32[1,24]{1,0:T(1,128)}, u32[]{:S(2)}) copy-start(f32[1,24]{1,0:T(1,128)} %get-tuple-element.70) | copy-start | bytes 292
  112.7 26.8 %copy-start.11 = (f32[1,24]{1,0:T(1,128)S(1)}, f32[1,24]{1,0:T(1,128)}, u32[]{:S(2)}) copy-start(f32[1,24]{1,0:T(1,128)} %get-tuple-element.67) | copy-start | bytes 292
  112.7 26.8 %copy-start.12 = (f32[1,24]{1,0:T(1,128)S(1)}, f32[1,24]{1,0:T(1,128)}, u32[]{:S(2)}) copy-start(f32[1,24]{1,0:T(1,128)} %get-tuple-element.68) | copy-start | bytes 292
  112.7 26.8 %copy-start.13 = (f32[1,24]{1,0:T(1,128)S(1)}, f32[1,24]{1,0:T(1,128)}, u32[]{:S(2)}) copy-start(f32[1,24]{1,0:T(1,128)} %get-tuple-element.65) | copy-start | bytes 292
  112.7 26.8 %copy-start.14 = (f32[1,24]{1,0:T(1,128)S(1)}, f32[1,24]{1,0:T(1,128)}, u32[]{:S(2)}) copy-start(f32[1,24]{1,0:T(1,128)} %get-tuple-element.66) | copy-start | bytes 292
  130.5 26.1 %all-to-all-start = ((f32[32,16,128]{2,1,0:T(8,128)}), f32[32,16,128]{2,1,0:T(8,128)S(1)}, u32[]{:S(2)}, u32[]{:S(2)}) async-start(f32[32,16,128]{2,1,0:T(8,128)} %bitcast.13), calls=%async_computation | async-start | bytes 524288 | tf_op jit(solution)/shard_map/all_to_all | solution.py:143
  159.9 3.2 %copy-start.1 = (f32[256,576]{1,0:T(8,128)S(1)}, f32[256,576]{1,0:T(8,128)}, u32[]{:S(2)}) copy-start(f32[256,576]{1,0:T(8,128)} %mul.3480) | copy-start | bytes 1769476
  183.2 25.1 %all-to-all-start.1 = ((f32[32,16,128]{2,1,0:T(8,128)}), f32[32,16,128]{2,1,0:T(8,128)S(1)}, u32[]{:S(2)}, u32[]{:S(2)}) async-start(f32[32,16,128]{2,1,0:T(8,128)} %constant_dynamic-update-slice_fusion), calls=%async_computation.1 | async-start | bytes 524288 | tf_op jit(solution)/shard_map/all_to_all | solution.py:163
